TPU v7x, 512 devices: a whole 4x4x16 slice. The times are simulated.
512 devices in a mesh: segment: 8 (over y, core), rows: 16 (over z), dp: 4 (over x).
Axes of the slice: x: 4, y: 4, z: 16, core: 2. Of those that a mesh axis runs over, the one named last changes fastest.
Arguments:
- clips: bfloat16 [4, 4, 4, 128, 8, 128], P(None, 'dp', None, 'rows'), may hold values from -80 to 80
- lengths: int32 [4, 4], P(None, 'dp'), may hold values from 1 to 4, as said below
- conv_weight: bfloat16 [8, 3456, 128], P('segment'), may hold values from -0.109375 to 0.109375
- norm_gain: float32 [8, 128], P('segment'), may hold values from 0.5 to 2
- norm_shift: float32 [8, 128], P('segment'), may hold values from -1 to 1
- conv_bias: float32 [8, 128], P('segment'), may hold values from -3 to 3
- cotangent: bfloat16 [8, 4, 4, 4, 128, 8, 128], P('segment', None, 'dp', None, 'rows'), may hold values from -6 to 6
Outputs:
- stash: bfloat16 [8, 4, 4, 4, 128, 8, 128], P('segment', None, 'dp', None, 'rows')
- weight_grad: float32 [8, 3456, 128], P('segment')
Inputs may be any that keep to these rules, and one draw needn't show every extreme that they name: lengths[m, clip] real frames lead each clip; the frames after them are padding; some clip has all 4 frames.
All inputs are finite; a program needn't handle non-finite values.
Results may differ from a plain program's by a relative error of at most 0.009.
Values may be sent and summed in bfloat16 or wider, within the bound.
A program may use at most 64 MiB of HBM per device.

v0:
```python
import math
import jax
import jax.numpy as jnp
from jax import lax
from jax.sharding import PartitionSpec as P

GROUPS = 32
eps = 1e-06


def extended_2(cells, sides, width):
    for axis, dim in sides:
        count = lax.axis_size(axis)
        ends = count - 1
        head = lax.slice_in_dim(cells, 0, width, axis=dim)
        tail = lax.slice_in_dim(cells, cells.shape[dim] - width, cells.shape[dim], axis=dim)
        cells = jnp.concatenate(
            [
                lax.ppermute(tail, axis, [(i, (i + 1) % count) for i in range(ends)]),
                cells,
                lax.ppermute(head, axis, [((i + 1) % count, i) for i in range(ends)]),
            ],
            axis=dim,
        )
    return cells


def passed_along(block, axis, distance):
    devices = range(lax.axis_size(axis))
    route = [(i - distance, i) for i in devices if i - distance in devices]
    return lax.ppermute(block, axis, route)


def statistics(values, frame_mask, length, height):
    clip_count, frames, rows_here, cols, chans = values.shape
    sub = chans // GROUPS
    grouped = values.reshape(clip_count, frames, rows_here, cols, GROUPS, sub)
    mask_six = frame_mask[:, :, :, :, :, None]
    count = (length * (height * cols * sub)).astype(jnp.float32)[:, None]
    total = lax.psum(jnp.sum(grouped * mask_six, axis=(1, 2, 3, 5)), "rows")
    mean = total / count
    centered = grouped - mean[:, None, None, None, :, None]
    spread = lax.psum(jnp.sum(centered * centered * mask_six, axis=(1, 2, 3, 5)), "rows")
    var = spread / count
    rstd = lax.rsqrt(var + eps)
    mean_chan = jnp.repeat(mean, sub, axis=-1)[:, None, None, None, :]
    rstd_chan = jnp.repeat(rstd, sub, axis=-1)[:, None, None, None, :]
    return (mean_chan, rstd_chan)


def block(current, length, weight, gain, shift, bias, height):
    clip_count, frames, rows_here, cols, chans = current.shape
    values = current.astype(jnp.float32)
    frame_mask = (jnp.arange(frames)[None, :] < length[:, None]).astype(jnp.float32)[
        :, :, None, None, None
    ]
    mean_chan, rstd_chan = statistics(values, frame_mask, length, height)
    hidden = jax.nn.silu((values - mean_chan) * rstd_chan * gain + shift).astype(jnp.bfloat16)
    extended = extended_2(hidden, (("rows", 2),), 1)
    padded = jnp.pad(extended, ((0, 0), (0, 0), (0, 0), (1, 1), (0, 0)))
    padded = jnp.concatenate([padded[:, :1], padded[:, :1], padded], axis=1)
    pieces = []
    for tap_t in range(3):
        for tap_h in range(3):
            for tap_w in range(3):
                pieces.append(
                    padded[
                        :,
                        tap_t : tap_t + frames,
                        tap_h : tap_h + rows_here,
                        tap_w : tap_w + cols,
                        :,
                    ]
                )
    patches = jnp.concatenate(pieces, axis=-1).reshape(-1, 27 * chans)
    conv = jnp.dot(patches, weight, preferred_element_type=jnp.float32).reshape(values.shape)
    result = ((values + conv + bias) * frame_mask).astype(jnp.bfloat16)
    return (result, patches, frame_mask.astype(jnp.bfloat16))


def per_device(clips, lengths, conv_weight, norm_gain, norm_shift, conv_bias, cotangent):
    segments = lax.axis_size("segment")
    segment_id = lax.axis_index("segment")
    micro = clips.shape[0]
    frames = clips.shape[2]
    cols = clips.shape[4]
    chans = clips.shape[5]
    height = clips.shape[3] * lax.axis_size("rows")
    weight = conv_weight[0]
    gain = norm_gain[0]
    shift = norm_shift[0]
    bias = conv_bias[0]
    cot_all = cotangent[0]
    total_cells = micro * clips.shape[1] * lax.axis_size("dp") * frames * height * cols
    factor = 1.0 / math.sqrt(total_cells)

    def tick(step, carry):
        arrived, stash, grads = carry
        which = step - segment_id
        valid = (which >= 0) & (which < micro)
        slot = jnp.clip(which, 0, micro - 1)
        fresh = lax.dynamic_index_in_dim(
            clips, jnp.clip(step, 0, micro - 1).astype(jnp.int32), 0, keepdims=False
        )
        current = jnp.where(segment_id == 0, fresh, arrived)
        length = lax.dynamic_index_in_dim(lengths, slot, 0, keepdims=False)
        result, patches, mask_five = block(current, length, weight, gain, shift, bias, height)
        cot_now = lax.dynamic_index_in_dim(cot_all, slot, 0, keepdims=False)
        masked = (cot_now * mask_five).reshape(-1, chans)
        term = lax.dot_general(
            patches, masked, (((0,), (0,)), ((), ())), preferred_element_type=jnp.float32
        )
        grads = grads + jnp.where(valid, term, 0.0)
        previous = lax.dynamic_index_in_dim(stash, slot, 0, keepdims=False)
        stash = lax.dynamic_update_index_in_dim(stash, jnp.where(valid, result, previous), slot, 0)
        arrived = passed_along(result, "segment", 1)
        return (arrived, stash, grads)

    start = (
        jnp.zeros(clips.shape[1:], jnp.bfloat16),
        jnp.zeros(clips.shape, jnp.bfloat16),
        jnp.zeros((27 * chans, chans), jnp.float32),
    )
    arrived, stash, grads = lax.fori_loop(0, micro + segments - 1, tick, start)
    grads = lax.psum(grads, ("rows", "dp")) * factor
    return (stash[None], grads[None])


def solution(mesh):
    in_specs = (
        P(None, "dp", None, "rows", None, None),
        P(None, "dp"),
        P("segment", None, None),
        P("segment", None),
        P("segment", None),
        P("segment", None),
        P("segment", None, "dp", None, "rows", None, None),
    )
    out_specs = (P("segment", None, "dp", None, "rows", None, None), P("segment", None, None))
    return jax.shard_map(
        per_device, mesh=mesh, in_specs=in_specs, out_specs=out_specs, check_vma=False
    )
```

profile of v0, /device:TPU:8, one launch (start us, length us, event | category | flops | bytes accessed | tf_op | source)
XLA Modules:
  0.0 1160.9 jit_solution(13718055022507466365)
XLA Ops:
  7.3 867.2 %while.20 = (s32[]{:T(128)}, bf16[1,4,8,8,128]{4,3,2,1,0:T(8,128)(2,1)S(1)}, bf16[4,1,4,8,8,128]{5,4,3,2,1,0:T(8,128)(2,1)S(1)}, f32[3456,128]{1,0:T(8,128)S(1)}...) while((s32[]{:T(128)}, ...), condition=%wide.region_7.8_spmd.clone, body=%wide.region_0.7_spmd.clone.sunk | while | flops 457701504 | bytes 18060908 | solution.py:124
  10.4 36.5 %psum.40 = f32[1,32]{1,0:T(1,128)S(1)} all-reduce(f32[1,32]{1,0:T(1,128)S(1)} %bitcast.110), channel_id=1, replica_groups=mesh['segment'=8,'rows'=16,'dp'=4] {'rows'}, use_global_device_ids=true, to_apply=%region_3.3 | all-reduce | flops 32 | bytes 256 | tf_op jit(solution)/shard_map/while/body/eval_jaxpr/psum | solution.py:40
  48.0 27.0 %psum.41 = f32[1,32]{1,0:T(1,128)S(1)} all-reduce(f32[1,32]{1,0:T(1,128)S(1)} %bitcast.109), channel_id=1, replica_groups=mesh['segment'=8,'rows'=16,'dp'=4] {'rows'}, use_global_device_ids=true, to_apply=%region_6.6 | all-reduce | flops 32 | bytes 256 | tf_op jit(solution)/shard_map/while/body/eval_jaxpr/psum | solution.py:43
  77.3 4.5 collective-permute-start.1
  85.6 1.9 collective-permute-start.2
  87.5 2.3 fusion.108
  89.8 1.4 collective-permute-done.2
  94.2 30.5 %psum.40 = f32[1,32]{1,0:T(1,128)S(1)} all-reduce(f32[1,32]{1,0:T(1,128)S(1)} %bitcast.110), channel_id=1, replica_groups=mesh['segment'=8,'rows'=16,'dp'=4] {'rows'}, use_global_device_ids=true, to_apply=%region_3.3 | all-reduce | flops 32 | bytes 256 | tf_op jit(solution)/shard_map/while/body/eval_jaxpr/psum | solution.py:40
  125.8 29.1 %psum.41 = f32[1,32]{1,0:T(1,128)S(1)} all-reduce(f32[1,32]{1,0:T(1,128)S(1)} %bitcast.109), channel_id=1, replica_groups=mesh['segment'=8,'rows'=16,'dp'=4] {'rows'}, use_global_device_ids=true, to_apply=%region_6.6 | all-reduce | flops 32 | bytes 256 | tf_op jit(solution)/shard_map/while/body/eval_jaxpr/psum | solution.py:43
  157.2 4.5 collective-permute-start.1
  165.4 1.9 collective-permute-start.2
  167.3 2.3 fusion.108
  169.6 1.4 collective-permute-done.2
  174.0 29.3 %psum.40 = f32[1,32]{1,0:T(1,128)S(1)} all-reduce(f32[1,32]{1,0:T(1,128)S(1)} %bitcast.110), channel_id=1, replica_groups=mesh['segment'=8,'rows'=16,'dp'=4] {'rows'}, use_global_device_ids=true, to_apply=%region_3.3 | all-reduce | flops 32 | bytes 256 | tf_op jit(solution)/shard_map/while/body/eval_jaxpr/psum | solution.py:40
  204.5 28.3 %psum.41 = f32[1,32]{1,0:T(1,128)S(1)} all-reduce(f32[1,32]{1,0:T(1,128)S(1)} %bitcast.109), channel_id=1, replica_groups=mesh['segment'=8,'rows'=16,'dp'=4] {'rows'}, use_global_device_ids=true, to_apply=%region_6.6 | all-reduce | flops 32 | bytes 256 | tf_op jit(solution)/shard_map/while/body/eval_jaxpr/psum | solution.py:43
  235.0 4.5 collective-permute-start.1
  243.2 1.9 collective-permute-start.2
  245.2 2.3 fusion.108
  247.4 1.4 collective-permute-done.2
  251.8 29.3 %psum.40 = f32[1,32]{1,0:T(1,128)S(1)} all-reduce(f32[1,32]{1,0:T(1,128)S(1)} %bitcast.110), channel_id=1, replica_groups=mesh['segment'=8,'rows'=16,'dp'=4] {'rows'}, use_global_device_ids=true, to_apply=%region_3.3 | all-reduce | flops 32 | bytes 256 | tf_op jit(solution)/shard_map/while/body/eval_jaxpr/psum | solution.py:40
  282.3 29.0 %psum.41 = f32[1,32]{1,0:T(1,128)S(1)} all-reduce(f32[1,32]{1,0:T(1,128)S(1)} %bitcast.109), channel_id=1, replica_groups=mesh['segment'=8,'rows'=16,'dp'=4] {'rows'}, use_global_device_ids=true, to_apply=%region_6.6 | all-reduce | flops 32 | bytes 256 | tf_op jit(solution)/shard_map/while/body/eval_jaxpr/psum | solution.py:43
  313.6 4.5 collective-permute-start.1
  321.8 1.9 collective-permute-start.2
  323.8 2.3 fusion.108
  330.4 29.3 %psum.40 = f32[1,32]{1,0:T(1,128)S(1)} all-reduce(f32[1,32]{1,0:T(1,128)S(1)} %bitcast.110), channel_id=1, replica_groups=mesh['segment'=8,'rows'=16,'dp'=4] {'rows'}, use_global_device_ids=true, to_apply=%region_3.3 | all-reduce | flops 32 | bytes 256 | tf_op jit(solution)/shard_map/while/body/eval_jaxpr/psum | solution.py:40
  360.9 28.2 %psum.41 = f32[1,32]{1,0:T(1,128)S(1)} all-reduce(f32[1,32]{1,0:T(1,128)S(1)} %bitcast.109), channel_id=1, replica_groups=mesh['segment'=8,'rows'=16,'dp'=4] {'rows'}, use_global_device_ids=true, to_apply=%region_6.6 | all-reduce | flops 32 | bytes 256 | tf_op jit(solution)/shard_map/while/body/eval_jaxpr/psum | solution.py:43
  391.4 4.5 collective-permute-start.1
  399.7 1.9 collective-permute-start.2
  401.6 2.3 fusion.108
  403.9 1.4 collective-permute-done.2
  408.3 29.3 %psum.40 = f32[1,32]{1,0:T(1,128)S(1)} all-reduce(f32[1,32]{1,0:T(1,128)S(1)} %bitcast.110), channel_id=1, replica_groups=mesh['segment'=8,'rows'=16,'dp'=4] {'rows'}, use_global_device_ids=true, to_apply=%region_3.3 | all-reduce | flops 32 | bytes 256 | tf_op jit(solution)/shard_map/while/body/eval_jaxpr/psum | solution.py:40
  438.8 29.0 %psum.41 = f32[1,32]{1,0:T(1,128)S(1)} all-reduce(f32[1,32]{1,0:T(1,128)S(1)} %bitcast.109), channel_id=1, replica_groups=mesh['segment'=8,'rows'=16,'dp'=4] {'rows'}, use_global_device_ids=true, to_apply=%region_6.6 | all-reduce | flops 32 | bytes 256 | tf_op jit(solution)/shard_map/while/body/eval_jaxpr/psum | solution.py:43
  470.0 4.5 collective-permute-start.1
  478.3 1.9 collective-permute-start.2
  480.2 2.3 fusion.108
  486.9 29.3 %psum.40 = f32[1,32]{1,0:T(1,128)S(1)} all-reduce(f32[1,32]{1,0:T(1,128)S(1)} %bitcast.110), channel_id=1, replica_groups=mesh['segment'=8,'rows'=16,'dp'=4] {'rows'}, use_global_device_ids=true, to_apply=%region_3.3 | all-reduce | flops 32 | bytes 256 | tf_op jit(solution)/shard_map/while/body/eval_jaxpr/psum | solution.py:40
  517.4 28.2 %psum.41 = f32[1,32]{1,0:T(1,128)S(1)} all-reduce(f32[1,32]{1,0:T(1,128)S(1)} %bitcast.109), channel_id=1, replica_groups=mesh['segment'=8,'rows'=16,'dp'=4] {'rows'}, use_global_device_ids=true, to_apply=%region_6.6 | all-reduce | flops 32 | bytes 256 | tf_op jit(solution)/shard_map/while/body/eval_jaxpr/psum | solution.py:43
  547.9 4.5 collective-permute-start.1
  556.1 1.9 collective-permute-start.2
  558.0 2.3 fusion.108
  564.7 29.3 %psum.40 = f32[1,32]{1,0:T(1,128)S(1)} all-reduce(f32[1,32]{1,0:T(1,128)S(1)} %bitcast.110), channel_id=1, replica_groups=mesh['segment'=8,'rows'=16,'dp'=4] {'rows'}, use_global_device_ids=true, to_apply=%region_3.3 | all-reduce | flops 32 | bytes 256 | tf_op jit(solution)/shard_map/while/body/eval_jaxpr/psum | solution.py:40
  595.2 29.0 %psum.41 = f32[1,32]{1,0:T(1,128)S(1)} all-reduce(f32[1,32]{1,0:T(1,128)S(1)} %bitcast.109), channel_id=1, replica_groups=mesh['segment'=8,'rows'=16,'dp'=4] {'rows'}, use_global_device_ids=true, to_apply=%region_6.6 | all-reduce | flops 32 | bytes 256 | tf_op jit(solution)/shard_map/while/body/eval_jaxpr/psum | solution.py:43
  626.5 4.5 collective-permute-start.1
  634.7 1.9 collective-permute-start.2
  636.6 2.3 fusion.108
  638.9 1.4 collective-permute-done.2
  643.3 29.3 %psum.40 = f32[1,32]{1,0:T(1,128)S(1)} all-reduce(f32[1,32]{1,0:T(1,128)S(1)} %bitcast.110), channel_id=1, replica_groups=mesh['segment'=8,'rows'=16,'dp'=4] {'rows'}, use_global_device_ids=true, to_apply=%region_3.3 | all-reduce | flops 32 | bytes 256 | tf_op jit(solution)/shard_map/while/body/eval_jaxpr/psum | solution.py:40
  673.8 28.2 %psum.41 = f32[1,32]{1,0:T(1,128)S(1)} all-reduce(f32[1,32]{1,0:T(1,128)S(1)} %bitcast.109), channel_id=1, replica_groups=mesh['segment'=8,'rows'=16,'dp'=4] {'rows'}, use_global_device_ids=true, to_apply=%region_6.6 | all-reduce | flops 32 | bytes 256 | tf_op jit(solution)/shard_map/while/body/eval_jaxpr/psum | solution.py:43
  704.3 4.5 collective-permute-start.1
  712.5 1.9 collective-permute-start.2
  714.5 2.3 fusion.108
  716.7 1.4 collective-permute-done.2
  721.1 29.3 %psum.40 = f32[1,32]{1,0:T(1,128)S(1)} all-reduce(f32[1,32]{1,0:T(1,128)S(1)} %bitcast.110), channel_id=1, replica_groups=mesh['segment'=8,'rows'=16,'dp'=4] {'rows'}, use_global_device_ids=true, to_apply=%region_3.3 | all-reduce | flops 32 | bytes 256 | tf_op jit(solution)/shard_map/while/body/eval_jaxpr/psum | solution.py:40
  751.6 29.0 %psum.41 = f32[1,32]{1,0:T(1,128)S(1)} all-reduce(f32[1,32]{1,0:T(1,128)S(1)} %bitcast.109), channel_id=1, replica_groups=mesh['segment'=8,'rows'=16,'dp'=4] {'rows'}, use_global_device_ids=true, to_apply=%region_6.6 | all-reduce | flops 32 | bytes 256 | tf_op jit(solution)/shard_map/while/body/eval_jaxpr/psum | solution.py:43
  782.9 4.5 collective-permute-start.1
  791.1 1.9 collective-permute-start.2
  793.1 2.3 fusion.108
  799.7 29.3 %psum.40 = f32[1,32]{1,0:T(1,128)S(1)} all-reduce(f32[1,32]{1,0:T(1,128)S(1)} %bitcast.110), channel_id=1, replica_groups=mesh['segment'=8,'rows'=16,'dp'=4] {'rows'}, use_global_device_ids=true, to_apply=%region_3.3 | all-reduce | flops 32 | bytes 256 | tf_op jit(solution)/shard_map/while/body/eval_jaxpr/psum | solution.py:40
  830.2 28.2 %psum.41 = f32[1,32]{1,0:T(1,128)S(1)} all-reduce(f32[1,32]{1,0:T(1,128)S(1)} %bitcast.109), channel_id=1, replica_groups=mesh['segment'=8,'rows'=16,'dp'=4] {'rows'}, use_global_device_ids=true, to_apply=%region_6.6 | all-reduce | flops 32 | bytes 256 | tf_op jit(solution)/shard_map/while/body/eval_jaxpr/psum | solution.py:43
  860.7 4.5 collective-permute-start.1
  869.0 1.9 collective-permute-start.2
  870.9 2.3 fusion.108
  875.8 275.4 %all-reduce.3.cloned.1.call-done = f32[3456,128]{1,0:T(8,128)} async-done(((f32[3456,128]{1,0:T(8,128)}), f32[3456,128]{1,0:T(8,128)}) %all-reduce.3.cloned.1.call-update) | async-done | bytes 1769488 | tf_op jit(solution)/shard_map/psum | solution.py:125
  1151.2 2.8 multiply_bitcast_fusion
  (674 shorter events, 109.7 us)
Async XLA Ops:
  7.2 1144.0 %all-reduce.3.cloned.1.call-start = ((), (), s32[]{:S(2)}) async-start(), calls=%async_computation | async-start | bytes 3538944 | tf_op jit(solution)/shard_map/psum | solution.py:125
  76.0 6.5 collective-permute-start
  77.3 5.9 collective-permute-start.1
  83.5 0.7 copy-start.3
  83.7 1.2 copy-start
  83.7 1.2 copy-start.5
  85.6 5.6 collective-permute-start.2
  155.9 6.5 collective-permute-start
  157.2 5.9 collective-permute-start.1
  163.4 0.7 copy-start.3
  163.6 1.2 copy-start
  163.6 1.2 copy-start.5
  165.4 5.6 collective-permute-start.2
  233.7 6.5 collective-permute-start
  235.0 5.9 collective-permute-start.1
  241.2 0.7 copy-start.3
  241.4 1.2 copy-start
  241.4 1.2 copy-start.5
  243.2 5.6 collective-permute-start.2
  312.3 6.5 collective-permute-start
  313.6 5.9 collective-permute-start.1
  319.8 0.7 copy-start.3
  320.0 1.2 copy-start
  320.0 1.2 copy-start.5
  321.8 5.6 collective-permute-start.2
  390.1 6.5 collective-permute-start
  391.4 5.9 collective-permute-start.1
  397.7 0.7 copy-start.3
  397.8 1.2 copy-start
  397.8 1.2 copy-start.5
  399.7 5.6 collective-permute-start.2
  468.7 6.5 collective-permute-start
  470.0 5.9 collective-permute-start.1
  476.3 0.7 copy-start.3
  476.4 1.2 copy-start
  476.4 1.2 copy-start.5
  478.3 5.6 collective-permute-start.2
  546.6 6.5 collective-permute-start
  547.9 5.9 collective-permute-start.1
  554.3 1.2 copy-start
  554.3 1.2 copy-start.5
  556.1 5.6 collective-permute-start.2
  625.2 6.5 collective-permute-start
  626.5 5.9 collective-permute-start.1
  632.9 1.2 copy-start
  632.9 1.2 copy-start.5
  634.7 5.6 collective-permute-start.2
  703.0 6.5 collective-permute-start
  704.3 5.9 collective-permute-start.1
  710.7 1.2 copy-start
  710.7 1.2 copy-start.5
  712.5 5.6 collective-permute-start.2
  781.6 6.5 collective-permute-start
  782.9 5.9 collective-permute-start.1
  789.3 1.2 copy-start
  789.3 1.2 copy-start.5
  791.1 5.6 collective-permute-start.2
  859.4 6.5 collective-permute-start
  860.7 5.9 collective-permute-start.1
  867.1 1.2 copy-start
  867.1 1.2 copy-start.5
  869.0 5.6 collective-permute-start.2
  874.5 1.2 copy-start.1
  874.5 279.5 %copy-start.2 = (bf16[4,1,4,8,8,128]{5,4,3,2,1,0:T(8,128)(2,1)}, bf16[4,1,4,8,8,128]{5,4,3,2,1,0:T(8,128)(2,1)S(1)}, u32[]{:S(2)}) copy-start(bf16[4,1,4,8,8,128]{5,4,3,2,1,0:T(8,128)(2,1)S(1)} %get-tuple-element.295) | copy-start | bytes 786436
  (16 other events, 11.4 us)
Sparse Core Ops, SparseCore 0:
  875.9 275.2 all-reduce.2
where the time goes:
time: 1160 us
  blocking collectives  644 us (56%)
  waiting for transfers between devices  299 us (26%)
  starting transfers between devices  85.4 us (7%)
  other arithmetic  58.3 us (5%)
  matrix products  32.1 us (3%)
  local copies, waits for them, and re-layouts  17.7 us (2%)
  between operations  14.1 us (1%)
    psum x11, blocking collectives, statistics(): total = lax.psum(jnp.sum(grouped * mask_six, axis=(1, 2, 3, 5)), 'rows')  331 us
    psum x11, blocking collectives, statistics(): lax.psum(jnp.sum(centered * centered * mask_six, axis=(1, 2, 3, 5)), 'rows')  313 us
    psum x1, waiting for transfers between devices, per_device(): grads = lax.psum(grads, ('rows', 'dp')) * factor  275 us
    ppermute x11, starting transfers between devices, extended_2(): lax.ppermute(tail, axis, [(i, (i + 1) % count) for i in range(ends)])  50 us
    dot_general x11, matrix products, tick(): lax.dot_general(patches, masked, (((0,), (0,)), ((), ())), preferred_elem...  24.9 us
  transfers between devices with their start and end apart: 34, of which 23 were waited for; matrix products, arithmetic and copies ran while one was open for 3% of the time, Pallas kernels for 0%

commit v1 on v0

--- a/solution.py
+++ b/solution.py
@@ -6,6 +6,10 @@
 
 GROUPS = 32
 eps = 1e-06
+
+
+def sides_draw(x_in):
+    return lax.psum(lax.psum(x_in, "dp"), "rows")
 
 
 def extended_2(cells, sides, width):
@@ -122,7 +126,7 @@
         jnp.zeros((27 * chans, chans), jnp.float32),
     )
     arrived, stash, grads = lax.fori_loop(0, micro + segments - 1, tick, start)
-    grads = lax.psum(grads, ("rows", "dp")) * factor
+    grads = sides_draw(grads) * factor
     return (stash[None], grads[None])
 
 

time: 1160 us -> 1100 us (0.948)
  the two profiles are of different devices: /device:TPU:8 before, /device:TPU:2 now
where the time goes in v1:
time: 1100 us
  blocking collectives  643 us (58%)
  waiting for transfers between devices  236 us (21%)
  starting transfers between devices  84.6 us (8%)
  other arithmetic  58.4 us (5%)
  matrix products  32.1 us (3%)
  local copies, waits for them, and re-layouts  17.7 us (2%)
  between operations  14.1 us (1%)
    psum x11, blocking collectives, statistics(): total = lax.psum(jnp.sum(grouped * mask_six, axis=(1, 2, 3, 5)), 'rows')  330 us
    psum x11, blocking collectives, statistics(): lax.psum(jnp.sum(centered * centered * mask_six, axis=(1, 2, 3, 5)), 'rows')  313 us
    psum x2, waiting for transfers between devices, sides_draw(): return lax.psum(lax.psum(x_in, 'dp'), 'rows')  228 us
    ppermute x11, starting transfers between devices, extended_2(): lax.ppermute(tail, axis, [(i, (i + 1) % count) for i in range(ends)])  50 us
    dot_general x11, matrix products, tick(): lax.dot_general(patches, masked, (((0,), (0,)), ((), ())), preferred_elem...  24.9 us
  transfers between devices with their start and end apart: 35, of which 13 were waited for; matrix products, arithmetic and copies ran while one was open for 3% of the time, Pallas kernels for 0%

profile of v1, /device:TPU:2, one launch (start us, length us, event | category | flops | bytes accessed | tf_op | source)
XLA Modules:
  0.0 1097.5 jit_solution(11393954254351184470)
XLA Ops:
  7.3 850.9 %while.20 = (s32[]{:T(128)}, bf16[1,4,8,8,128]{4,3,2,1,0:T(8,128)(2,1)S(1)}, bf16[4,1,4,8,8,128]{5,4,3,2,1,0:T(8,128)(2,1)S(1)}, f32[3456,128]{1,0:T(8,128)S(1)}...) while((s32[]{:T(128)}, ...), condition=%wide.region_7.8_spmd.clone, body=%wide.region_0.7_spmd.clone.sunk | while | flops 457701504 | bytes 18060908 | solution.py:128
  10.4 36.5 %psum.48 = f32[1,32]{1,0:T(1,128)S(1)} all-reduce(f32[1,32]{1,0:T(1,128)S(1)} %bitcast.110), channel_id=1, replica_groups=mesh['segment'=8,'rows'=16,'dp'=4] {'rows'}, use_global_device_ids=true, to_apply=%region_3.3 | all-reduce | flops 32 | bytes 256 | tf_op jit(solution)/shard_map/while/body/eval_jaxpr/psum | solution.py:44
  48.0 27.0 %psum.49 = f32[1,32]{1,0:T(1,128)S(1)} all-reduce(f32[1,32]{1,0:T(1,128)S(1)} %bitcast.109), channel_id=1, replica_groups=mesh['segment'=8,'rows'=16,'dp'=4] {'rows'}, use_global_device_ids=true, to_apply=%region_6.6 | all-reduce | flops 32 | bytes 256 | tf_op jit(solution)/shard_map/while/body/eval_jaxpr/psum | solution.py:47
  76.0 1.3 collective-permute-start
  77.3 4.5 collective-permute-start.1
  85.6 1.3 collective-permute-start.2
  86.9 2.3 fusion.108
  92.2 30.5 %psum.48 = f32[1,32]{1,0:T(1,128)S(1)} all-reduce(f32[1,32]{1,0:T(1,128)S(1)} %bitcast.110), channel_id=1, replica_groups=mesh['segment'=8,'rows'=16,'dp'=4] {'rows'}, use_global_device_ids=true, to_apply=%region_3.3 | all-reduce | flops 32 | bytes 256 | tf_op jit(solution)/shard_map/while/body/eval_jaxpr/psum | solution.py:44
  123.9 29.0 %psum.49 = f32[1,32]{1,0:T(1,128)S(1)} all-reduce(f32[1,32]{1,0:T(1,128)S(1)} %bitcast.109), channel_id=1, replica_groups=mesh['segment'=8,'rows'=16,'dp'=4] {'rows'}, use_global_device_ids=true, to_apply=%region_6.6 | all-reduce | flops 32 | bytes 256 | tf_op jit(solution)/shard_map/while/body/eval_jaxpr/psum | solution.py:47
  153.8 1.3 collective-permute-start
  155.1 4.5 collective-permute-start.1
  163.4 1.3 collective-permute-start.2
  164.7 2.3 fusion.108
  170.0 29.3 %psum.48 = f32[1,32]{1,0:T(1,128)S(1)} all-reduce(f32[1,32]{1,0:T(1,128)S(1)} %bitcast.110), channel_id=1, replica_groups=mesh['segment'=8,'rows'=16,'dp'=4] {'rows'}, use_global_device_ids=true, to_apply=%region_3.3 | all-reduce | flops 32 | bytes 256 | tf_op jit(solution)/shard_map/while/body/eval_jaxpr/psum | solution.py:44
  200.5 28.3 %psum.49 = f32[1,32]{1,0:T(1,128)S(1)} all-reduce(f32[1,32]{1,0:T(1,128)S(1)} %bitcast.109), channel_id=1, replica_groups=mesh['segment'=8,'rows'=16,'dp'=4] {'rows'}, use_global_device_ids=true, to_apply=%region_6.6 | all-reduce | flops 32 | bytes 256 | tf_op jit(solution)/shard_map/while/body/eval_jaxpr/psum | solution.py:47
  229.8 1.3 collective-permute-start
  231.1 4.5 collective-permute-start.1
  239.3 1.3 collective-permute-start.2
  240.6 2.3 fusion.108
  245.9 29.3 %psum.48 = f32[1,32]{1,0:T(1,128)S(1)} all-reduce(f32[1,32]{1,0:T(1,128)S(1)} %bitcast.110), channel_id=1, replica_groups=mesh['segment'=8,'rows'=16,'dp'=4] {'rows'}, use_global_device_ids=true, to_apply=%region_3.3 | all-reduce | flops 32 | bytes 256 | tf_op jit(solution)/shard_map/while/body/eval_jaxpr/psum | solution.py:44
  276.5 28.9 %psum.49 = f32[1,32]{1,0:T(1,128)S(1)} all-reduce(f32[1,32]{1,0:T(1,128)S(1)} %bitcast.109), channel_id=1, replica_groups=mesh['segment'=8,'rows'=16,'dp'=4] {'rows'}, use_global_device_ids=true, to_apply=%region_6.6 | all-reduce | flops 32 | bytes 256 | tf_op jit(solution)/shard_map/while/body/eval_jaxpr/psum | solution.py:47
  306.3 1.3 collective-permute-start
  307.6 4.5 collective-permute-start.1
  315.9 1.3 collective-permute-start.2
  317.2 2.3 fusion.108
  322.5 29.3 %psum.48 = f32[1,32]{1,0:T(1,128)S(1)} all-reduce(f32[1,32]{1,0:T(1,128)S(1)} %bitcast.110), channel_id=1, replica_groups=mesh['segment'=8,'rows'=16,'dp'=4] {'rows'}, use_global_device_ids=true, to_apply=%region_3.3 | all-reduce | flops 32 | bytes 256 | tf_op jit(solution)/shard_map/while/body/eval_jaxpr/psum | solution.py:44
  353.0 28.3 %psum.49 = f32[1,32]{1,0:T(1,128)S(1)} all-reduce(f32[1,32]{1,0:T(1,128)S(1)} %bitcast.109), channel_id=1, replica_groups=mesh['segment'=8,'rows'=16,'dp'=4] {'rows'}, use_global_device_ids=true, to_apply=%region_6.6 | all-reduce | flops 32 | bytes 256 | tf_op jit(solution)/shard_map/while/body/eval_jaxpr/psum | solution.py:47
  383.6 4.5 collective-permute-start.1
  391.8 1.3 collective-permute-start.2
  393.1 2.3 fusion.108
  398.4 29.3 %psum.48 = f32[1,32]{1,0:T(1,128)S(1)} all-reduce(f32[1,32]{1,0:T(1,128)S(1)} %bitcast.110), channel_id=1, replica_groups=mesh['segment'=8,'rows'=16,'dp'=4] {'rows'}, use_global_device_ids=true, to_apply=%region_3.3 | all-reduce | flops 32 | bytes 256 | tf_op jit(solution)/shard_map/while/body/eval_jaxpr/psum | solution.py:44
  428.9 29.0 %psum.49 = f32[1,32]{1,0:T(1,128)S(1)} all-reduce(f32[1,32]{1,0:T(1,128)S(1)} %bitcast.109), channel_id=1, replica_groups=mesh['segment'=8,'rows'=16,'dp'=4] {'rows'}, use_global_device_ids=true, to_apply=%region_6.6 | all-reduce | flops 32 | bytes 256 | tf_op jit(solution)/shard_map/while/body/eval_jaxpr/psum | solution.py:47
  458.9 1.3 collective-permute-start
  460.2 4.5 collective-permute-start.1
  468.5 1.3 collective-permute-start.2
  469.8 2.3 fusion.108
  475.1 29.3 %psum.48 = f32[1,32]{1,0:T(1,128)S(1)} all-reduce(f32[1,32]{1,0:T(1,128)S(1)} %bitcast.110), channel_id=1, replica_groups=mesh['segment'=8,'rows'=16,'dp'=4] {'rows'}, use_global_device_ids=true, to_apply=%region_3.3 | all-reduce | flops 32 | bytes 256 | tf_op jit(solution)/shard_map/while/body/eval_jaxpr/psum | solution.py:44
  505.6 28.2 %psum.49 = f32[1,32]{1,0:T(1,128)S(1)} all-reduce(f32[1,32]{1,0:T(1,128)S(1)} %bitcast.109), channel_id=1, replica_groups=mesh['segment'=8,'rows'=16,'dp'=4] {'rows'}, use_global_device_ids=true, to_apply=%region_6.6 | all-reduce | flops 32 | bytes 256 | tf_op jit(solution)/shard_map/while/body/eval_jaxpr/psum | solution.py:47
  536.1 4.5 collective-permute-start.1
  544.3 1.3 collective-permute-start.2
  545.6 2.3 fusion.108
  551.0 29.3 %psum.48 = f32[1,32]{1,0:T(1,128)S(1)} all-reduce(f32[1,32]{1,0:T(1,128)S(1)} %bitcast.110), channel_id=1, replica_groups=mesh['segment'=8,'rows'=16,'dp'=4] {'rows'}, use_global_device_ids=true, to_apply=%region_3.3 | all-reduce | flops 32 | bytes 256 | tf_op jit(solution)/shard_map/while/body/eval_jaxpr/psum | solution.py:44
  581.4 29.0 %psum.49 = f32[1,32]{1,0:T(1,128)S(1)} all-reduce(f32[1,32]{1,0:T(1,128)S(1)} %bitcast.109), channel_id=1, replica_groups=mesh['segment'=8,'rows'=16,'dp'=4] {'rows'}, use_global_device_ids=true, to_apply=%region_6.6 | all-reduce | flops 32 | bytes 256 | tf_op jit(solution)/shard_map/while/body/eval_jaxpr/psum | solution.py:47
  612.7 4.5 collective-permute-start.1
  621.0 1.3 collective-permute-start.2
  622.3 2.3 fusion.108
  627.6 29.3 %psum.48 = f32[1,32]{1,0:T(1,128)S(1)} all-reduce(f32[1,32]{1,0:T(1,128)S(1)} %bitcast.110), channel_id=1, replica_groups=mesh['segment'=8,'rows'=16,'dp'=4] {'rows'}, use_global_device_ids=true, to_apply=%region_3.3 | all-reduce | flops 32 | bytes 256 | tf_op jit(solution)/shard_map/while/body/eval_jaxpr/psum | solution.py:44
  658.1 28.2 %psum.49 = f32[1,32]{1,0:T(1,128)S(1)} all-reduce(f32[1,32]{1,0:T(1,128)S(1)} %bitcast.109), channel_id=1, replica_groups=mesh['segment'=8,'rows'=16,'dp'=4] {'rows'}, use_global_device_ids=true, to_apply=%region_6.6 | all-reduce | flops 32 | bytes 256 | tf_op jit(solution)/shard_map/while/body/eval_jaxpr/psum | solution.py:47
  688.6 4.5 collective-permute-start.1
  696.8 2.8 collective-permute-start.2
  699.6 2.3 fusion.108
  704.9 29.0 %psum.48 = f32[1,32]{1,0:T(1,128)S(1)} all-reduce(f32[1,32]{1,0:T(1,128)S(1)} %bitcast.110), channel_id=1, replica_groups=mesh['segment'=8,'rows'=16,'dp'=4] {'rows'}, use_global_device_ids=true, to_apply=%region_3.3 | all-reduce | flops 32 | bytes 256 | tf_op jit(solution)/shard_map/while/body/eval_jaxpr/psum | solution.py:44
  735.1 28.6 %psum.49 = f32[1,32]{1,0:T(1,128)S(1)} all-reduce(f32[1,32]{1,0:T(1,128)S(1)} %bitcast.109), channel_id=1, replica_groups=mesh['segment'=8,'rows'=16,'dp'=4] {'rows'}, use_global_device_ids=true, to_apply=%region_6.6 | all-reduce | flops 32 | bytes 256 | tf_op jit(solution)/shard_map/while/body/eval_jaxpr/psum | solution.py:47
  765.9 4.5 collective-permute-start.1
  774.2 3.9 collective-permute-start.2
  778.0 2.3 fusion.108
  783.4 29.0 %psum.48 = f32[1,32]{1,0:T(1,128)S(1)} all-reduce(f32[1,32]{1,0:T(1,128)S(1)} %bitcast.110), channel_id=1, replica_groups=mesh['segment'=8,'rows'=16,'dp'=4] {'rows'}, use_global_device_ids=true, to_apply=%region_3.3 | all-reduce | flops 32 | bytes 256 | tf_op jit(solution)/shard_map/while/body/eval_jaxpr/psum | solution.py:44
  813.6 28.5 %psum.49 = f32[1,32]{1,0:T(1,128)S(1)} all-reduce(f32[1,32]{1,0:T(1,128)S(1)} %bitcast.109), channel_id=1, replica_groups=mesh['segment'=8,'rows'=16,'dp'=4] {'rows'}, use_global_device_ids=true, to_apply=%region_6.6 | all-reduce | flops 32 | bytes 256 | tf_op jit(solution)/shard_map/while/body/eval_jaxpr/psum | solution.py:47
  844.3 4.5 collective-permute-start.1
  852.6 3.3 collective-permute-start.2
  855.9 2.3 fusion.108
  859.5 82.2 %all-reduce.4.cloned.1.call-done = f32[3456,128]{1,0:T(8,128)} async-done(((f32[3456,128]{1,0:T(8,128)}), f32[3456,128]{1,0:T(8,128)}) %all-reduce.4.cloned.1.call-update) | async-done | bytes 1769488 | tf_op jit(solution)/shard_map/psum | solution.py:12
  941.8 146.1 %all-reduce.6.cloned.1.call-done = f32[3456,128]{1,0:T(8,128)} async-done(((f32[3456,128]{1,0:T(8,128)}), f32[3456,128]{1,0:T(8,128)}) %all-reduce.6.cloned.1.call-update) | async-done | bytes 1769488 | tf_op jit(solution)/shard_map/psum | solution.py:12
  1087.8 2.8 multiply_bitcast_fusion
  (677 shorter events, 96.4 us)
Async XLA Ops:
  7.2 934.6 %all-reduce.4.cloned.1.call-start = ((), (), s32[]{:S(2)}) async-start(), calls=%async_computation | async-start | bytes 3538944 | tf_op jit(solution)/shard_map/psum | solution.py:12
  76.0 6.5 collective-permute-start
  77.3 5.9 collective-permute-start.1
  83.5 0.7 copy-start.3
  83.7 1.2 copy-start
  83.7 1.2 copy-start.5
  85.6 3.6 collective-permute-start.2
  153.8 6.5 collective-permute-start
  155.1 5.9 collective-permute-start.1
  161.4 0.7 copy-start.3
  161.6 1.2 copy-start
  161.6 1.2 copy-start.5
  163.4 3.6 collective-permute-start.2
  229.8 6.5 collective-permute-start
  231.1 5.9 collective-permute-start.1
  237.3 0.7 copy-start.3
  237.5 1.2 copy-start
  237.5 1.2 copy-start.5
  239.3 3.6 collective-permute-start.2
  306.3 6.5 collective-permute-start
  307.6 5.9 collective-permute-start.1
  314.0 1.2 copy-start
  314.1 1.2 copy-start.5
  315.9 3.6 collective-permute-start.2
  382.3 6.5 collective-permute-start
  383.6 5.9 collective-permute-start.1
  389.8 0.7 copy-start.3
  390.0 1.2 copy-start
  390.0 1.2 copy-start.5
  391.8 3.6 collective-permute-start.2
  458.9 6.5 collective-permute-start
  460.2 5.9 collective-permute-start.1
  466.6 1.2 copy-start
  466.6 1.2 copy-start.5
  468.5 3.6 collective-permute-start.2
  534.8 6.5 collective-permute-start
  536.1 5.9 collective-permute-start.1
  542.5 1.2 copy-start
  542.5 1.2 copy-start.5
  544.3 3.6 collective-permute-start.2
  611.4 6.5 collective-permute-start
  612.7 5.9 collective-permute-start.1
  618.9 0.7 copy-start.3
  619.1 1.2 copy-start
  619.1 1.2 copy-start.5
  621.0 3.6 collective-permute-start.2
  687.3 6.5 collective-permute-start
  688.6 5.9 collective-permute-start.1
  695.0 1.2 copy-start
  695.0 1.2 copy-start.5
  696.8 5.0 collective-permute-start.2
  764.6 6.5 collective-permute-start
  765.9 5.9 collective-permute-start.1
  772.3 1.2 copy-start
  772.4 1.2 copy-start.5
  774.2 6.1 collective-permute-start.2
  843.0 6.5 collective-permute-start
  844.3 5.9 collective-permute-start.1
  850.7 1.2 copy-start
  850.7 1.2 copy-start.5
  852.6 5.6 collective-permute-start.2
  858.2 1.2 copy-start.1
  858.2 83.5 %copy-start.2 = (bf16[4,1,4,8,8,128]{5,4,3,2,1,0:T(8,128)(2,1)}, bf16[4,1,4,8,8,128]{5,4,3,2,1,0:T(8,128)(2,1)S(1)}, u32[]{:S(2)}) copy-start(bf16[4,1,4,8,8,128]{5,4,3,2,1,0:T(8,128)(2,1)S(1)} %get-tuple-element.295) | copy-start | bytes 786436
  859.4 228.4 %all-reduce.6.cloned.1.call-start = ((), (), s32[]{:S(2)}) async-start(), calls=%async_computation.1 | async-start | bytes 3538944 | tf_op jit(solution)/shard_map/psum | solution.py:12
  (17 other events, 12.1 us)
Sparse Core Ops, SparseCore 0:
  859.6 82.1 all-reduce.3
  944.2 143.5 all-reduce.5
